TPU v7x, 512 devices: a whole 4x4x16 slice. The times are simulated.
512 devices in a mesh: pm: 2 (over y_lo), ka: 128 (over x, z, core), isdf: 2 (over y_hi).
Axes of the slice: x: 4, y: 4 (y_hi: 2, y_lo: 2; y = y_hi * 2 + y_lo), z: 16, core: 2. Of those that a mesh axis runs over, the one named last changes fastest.
Arguments:
- amplitudes: bfloat16 [2, 2, 2, 256, 64, 256], P('pm', None, None, 'ka'), may hold values from -6 to 6
- conduction: bfloat16 [2, 256, 256, 512], P(None, 'ka', None, 'isdf'), may hold values from -0.375 to 0.375
- valence: bfloat16 [2, 256, 64, 512], P(None, 'ka'), may hold values from -0.75 to 0.75
- energy: float32 [256, 64, 256], P('ka', None, 'isdf'), may hold values from 0.5 to 2.5
- screened: bfloat16 [4, 2, 512, 512], P(None, None, 'isdf'), may hold values from -0.59765625 to 0.59765625
- coulomb: float32 [512, 512], P(None, 'isdf'), may hold values from -0.03125 to 0.03125
- mirror: int32 [256], P('ka'), may hold values from 0 to 255, as said below
- transfer_class: int32 [256, 256], P('ka'), may hold values from 0 to 3, as said below
Outputs:
- response: bfloat16 [2, 2, 2, 256, 64, 256], P('pm', None, None, 'ka', None, 'isdf')
Inputs may be any that keep to these rules, and one draw needn't show every extreme that they name: mirror[mirror[k]] = k; a k-point of block j (the aligned block of 2 k-points that holds it) has its mirror in block 127 - j. transfer_class[k, k2] depends only on (k - k2) mod 256.
All inputs are finite; a program needn't handle non-finite values.
Results may differ from a plain program's by a relative error of at most 0.015.
Values may be sent and summed in bfloat16 or wider, within the bound.
A program may use at most 128 MiB of HBM per device.

v0:
```python
import jax
import jax.numpy as jnp
from jax import lax
from jax.sharding import PartitionSpec as P

REACH = 2
HIGHEST = lax.Precision.HIGHEST


def swapped(block, axis, apart):
    count = lax.axis_size(axis)
    route = []
    for low in range(count):
        high = low | 1 << apart
        if high != low and high < count:
            route += [(low, high), (high, low)]
    return lax.ppermute(block, axis, route)


def shifted(value, axis, by):
    size = lax.axis_size(axis)
    return lax.ppermute(value, axis, [(i, (i + by) % size) for i in range(size)])


def pair_einsum(pattern, left, right, conjugate):

    def single(first, second):
        return jnp.einsum(pattern, first, second, preferred_element_type=jnp.float32)

    if conjugate:
        real_part = single(left[0], right[0]) + single(left[1], right[1])
        imag_part = single(left[1], right[0]) - single(left[0], right[1])
    else:
        real_part = single(left[0], right[0]) - single(left[1], right[1])
        imag_part = single(left[0], right[1]) + single(left[1], right[0])
    return (real_part, imag_part)


def conjugated(field):
    return jnp.stack([field[:, 0], -field[:, 1]], axis=1)


def coefficients(vector, conduction):
    real_part, imag_part = pair_einsum(
        "bkvc,kcm->bkvm", (vector[:, 0], vector[:, 1]), (conduction[0], conduction[1]), False
    )
    return jnp.stack([real_part, imag_part], axis=1).astype(jnp.bfloat16)


def amp_bits(field):
    for bit_number in range(lax.axis_size("ka").bit_length() - 1):
        field = swapped(field, "ka", bit_number)
    return field


def result_bits(field):
    for bit_number in range(lax.axis_size("ka").bit_length() - 1):
        field = swapped(field, "ka", bit_number)
    return field


def by_mirror(field, local_mirror):
    index = local_mirror[None, None, :, None, None]
    return jnp.where(index == 0, field[:, :, 0:1], field[:, :, 1:2])


def per_device(amplitudes, conduction, valence, energy, screened, coulomb, mirror, transfer_class):
    pm_index = lax.axis_index("pm")
    ka_index = lax.axis_index("ka")
    isdf_index = lax.axis_index("isdf")
    ka_count = lax.axis_size("ka")
    kpoint_count = conduction.shape[1]
    mu_count = conduction.shape[3]
    point_count = valence.shape[3]
    cond_share = energy.shape[2]
    vector_count = amplitudes.shape[1]
    is_plus = pm_index == 0
    parity = jnp.where(is_plus, 1.0, -1.0).astype(jnp.float32)
    exchange_weight = jnp.where(is_plus, 4.0, 0.0).astype(jnp.float32)
    local_amps = amplitudes[0]
    partner_amps = swapped(local_amps, "pm", 0)
    partner_side = jnp.where(is_plus, partner_amps, local_amps)
    distant_side = amp_bits(partner_side)
    direct = jnp.where(is_plus, local_amps, partner_amps).astype(jnp.float32)
    local_mirror = mirror - (ka_count - 1 - ka_index) * kpoint_count
    flipped = conjugated(by_mirror(distant_side, local_mirror).astype(jnp.float32))
    vector = (direct + parity * flipped).astype(jnp.bfloat16)
    own_coef = coefficients(vector, conduction)
    valence_part = lax.dynamic_slice_in_dim(valence, isdf_index * mu_count, mu_count, 3)
    rho_real = jnp.einsum(
        "kvm,bkvm->bm", valence_part[0], own_coef[:, 0], preferred_element_type=jnp.float32
    )
    rho_real = rho_real + jnp.einsum(
        "kvm,bkvm->bm", valence_part[1], own_coef[:, 1], preferred_element_type=jnp.float32
    )
    rho_imag = jnp.einsum(
        "kvm,bkvm->bm", valence_part[0], own_coef[:, 1], preferred_element_type=jnp.float32
    )
    rho_imag = rho_imag - jnp.einsum(
        "kvm,bkvm->bm", valence_part[1], own_coef[:, 0], preferred_element_type=jnp.float32
    )
    density = jnp.stack([rho_real, rho_imag], axis=1)
    spread = jnp.einsum("nm,brm->brn", coulomb, density, precision=HIGHEST)
    spread = lax.psum(spread, ("ka", "isdf"))
    potential = lax.dynamic_slice_in_dim(spread, isdf_index * mu_count, mu_count, 2)
    class_ids = jnp.arange(screened.shape[0], dtype=jnp.int32)

    def accumulate(totals, coef_block, valence_block, source):
        pair_real, pair_imag = pair_einsum(
            "bqvm,qvn->bqmn",
            (coef_block[:, 0], coef_block[:, 1]),
            (valence_block[0], valence_block[1]),
            True,
        )
        pair_real = pair_real.astype(jnp.bfloat16)
        pair_imag = pair_imag.astype(jnp.bfloat16)
        classes = lax.dynamic_slice_in_dim(transfer_class, source * kpoint_count, kpoint_count, 1)
        selector = (classes[:, :, None] == class_ids).astype(jnp.bfloat16)
        total_real, total_imag = totals
        for visitor in range(kpoint_count):
            chosen = jnp.einsum(
                "kw,wrmn->rkmn", selector[:, visitor], screened, preferred_element_type=jnp.float32
            ).astype(jnp.bfloat16)
            screen_real = chosen[0][None].astype(jnp.float32)
            screen_imag = chosen[1][None].astype(jnp.float32)
            visit_real = pair_real[:, visitor][:, None].astype(jnp.float32)
            visit_imag = pair_imag[:, visitor][:, None].astype(jnp.float32)
            total_real = total_real + (screen_real * visit_real - screen_imag * visit_imag)
            total_imag = total_imag + (screen_real * visit_imag + screen_imag * visit_real)
        return (total_real, total_imag)

    payload = (vector, conduction, valence)

    def advance(moving, offset):
        return shifted((moving[0], moving[1], moving[2]), "ka", offset)

    def unpack(moving):
        return (coefficients(moving[0], moving[1]), moving[2])

    def visit(totals, moving, distance):
        coef_block, valence_block = unpack(moving)
        source = jnp.mod(ka_index + distance, ka_count)
        return accumulate(totals, coef_block, valence_block, source)

    zero_field = jnp.zeros((vector_count, kpoint_count, mu_count, point_count), jnp.float32)
    totals = accumulate((zero_field, zero_field), own_coef, valence, ka_index)
    below_item = payload
    for count_done in range(REACH):
        below_item = advance(below_item, 1)
        totals = visit(totals, below_item, -(count_done + 1))
    above_item = payload
    for count_done in range(REACH):
        above_item = advance(above_item, -1)
        totals = visit(totals, above_item, count_done + 1)
    sum_real = totals[0].astype(jnp.bfloat16)
    sum_imag = totals[1].astype(jnp.bfloat16)
    back_real, back_imag = pair_einsum(
        "bkmn,kvn->bkvm", (sum_real, sum_imag), (valence[0], valence[1]), False
    )
    potential_real = potential[:, 0][:, None, None, :]
    potential_imag = potential[:, 1][:, None, None, :]
    exchange_real = potential_real * valence_part[0] - potential_imag * valence_part[1]
    exchange_imag = potential_real * valence_part[1] + potential_imag * valence_part[0]
    field_real = (exchange_weight * exchange_real - back_real).astype(jnp.bfloat16)
    field_imag = (exchange_weight * exchange_imag - back_imag).astype(jnp.bfloat16)
    out_real, out_imag = pair_einsum(
        "bkvm,kcm->bkvc", (field_real, field_imag), (conduction[0], conduction[1]), True
    )
    partial_out = jnp.stack([out_real, out_imag], axis=1)
    summed = lax.psum_scatter(
        partial_out.astype(jnp.bfloat16), "isdf", scatter_dimension=4, tiled=True
    ).astype(jnp.float32)
    vector_part = lax.dynamic_slice_in_dim(vector, isdf_index * cond_share, cond_share, 4).astype(
        jnp.float32
    )
    channel_out = (energy[None, None] * vector_part + summed).astype(jnp.bfloat16)
    partner_out = swapped(channel_out, "pm", 0)
    blended = (
        0.5 * (partner_out.astype(jnp.float32) + parity * channel_out.astype(jnp.float32))
    ).astype(jnp.bfloat16)
    distant_out = result_bits(blended)
    reflected = conjugated(by_mirror(distant_out, local_mirror))
    result = jnp.where(is_plus, blended, reflected)
    return result[None]


def solution(mesh):
    return jax.shard_map(
        per_device,
        mesh=mesh,
        in_specs=(
            P("pm", None, None, "ka", None, None),
            P(None, "ka", None, "isdf"),
            P(None, "ka", None, None),
            P("ka", None, "isdf"),
            P(None, None, "isdf", None),
            P(None, "isdf"),
            P("ka"),
            P("ka", None),
        ),
        out_specs=P("pm", None, None, "ka", None, "isdf"),
        check_vma=False,
    )
```

profile of v0, /device:TPU:2, one launch (start us, length us, event | category | flops | bytes accessed | tf_op | source)
XLA Modules:
  0.0 1086.2 jit_solution(11353441118219177994)
XLA Ops:
  8.6 10.8 collective-permute-start.15
  21.3 5.8 collective-permute-start.16
  28.1 3.5 collective-permute-start
  32.8 3.2 copy.48
  59.1 3.0 fusion.87
  66.2 3.5 fusion.75
  78.0 6.5 collective-permute-done.2
  88.5 12.3 %collective-permute-done.3 = bf16[2,2,2,64,256]{4,3,0,2,1:T(8,128)(2,1)S(1)} collective-permute-done((bf16[2,2,2,64,256]{4,3,0,2,1:T(8,128)(2,1)S(1)}, bf16[2,2,2,64,256]{4,3,0,2,1:T(8,128)(2,1)S(1)}, u32[]{:S(2)}, u32[]{:S(2)}) %collective-permute-start.3) | collective-permute-done | bytes 262176 | tf_op jit(solution)/shard_map/ppermute | solution.py:17
  105.3 22.7 %collective-permute-done.4 = bf16[2,2,2,64,256]{4,3,0,2,1:T(8,128)(2,1)S(1)} collective-permute-done((bf16[2,2,2,64,256]{4,3,0,2,1:T(8,128)(2,1)S(1)}, bf16[2,2,2,64,256]{4,3,0,2,1:T(8,128)(2,1)S(1)}, u32[]{:S(2)}, u32[]{:S(2)}) %collective-permute-start.4) | collective-permute-done | bytes 262176 | tf_op jit(solution)/shard_map/ppermute | solution.py:17
  128.0 14.7 %collective-permute-start.5 = (bf16[2,2,2,64,256]{4,3,0,2,1:T(8,128)(2,1)S(1)}, bf16[2,2,2,64,256]{4,3,0,2,1:T(8,128)(2,1)S(1)}, u32[]{:S(2)}, u32[]{:S(2)}) collective-permute-start(bf16[2,2,2,64,256]{4,3,0,2,1:T(8,128)(2,1)S(1)} %collective-permute-done.4), channel_id=1, source_target_pairs={{0,32},{32,0},{2,34},{34,2},{4,36},{36,4},{6,38},{38,6},{8,40},{40... | collective-permute-start | bytes 786440 | tf_op jit(solution)/shard_map/ppermute | solution.py:17
  144.7 14.9 %collective-permute-done.5 = bf16[2,2,2,64,256]{4,3,0,2,1:T(8,128)(2,1)S(1)} collective-permute-done((bf16[2,2,2,64,256]{4,3,0,2,1:T(8,128)(2,1)S(1)}, bf16[2,2,2,64,256]{4,3,0,2,1:T(8,128)(2,1)S(1)}, u32[]{:S(2)}, u32[]{:S(2)}) %collective-permute-start.5) | collective-permute-done | bytes 262176 | tf_op jit(solution)/shard_map/ppermute | solution.py:17
  164.4 5.4 collective-permute-done.6
  169.8 4.2 collective-permute-start.7
  200.1 5.8 collective-permute-start.19
  207.9 5.8 collective-permute-start.18
  225.0 583.0 %psum.7 = f32[2,2,512]{2,1,0:T(2,128)S(1)} all-reduce(f32[2,2,512]{2,1,0:T(2,128)S(1)} %fusion.90), channel_id=1, replica_groups=mesh['pm'=2,'ka'=128,'isdf'=2] {'ka','isdf'}, use_global_device_ids=true, to_apply=%region_0.1 | all-reduce | flops 2048 | bytes 16384 | tf_op jit(solution)/shard_map/psum | solution.py:104
  842.2 5.3 collective-permute-start.17
  875.2 9.2 add_convert_fusion
  884.5 9.5 add_convert_fusion.1
  898.4 92.4 %reduce-scatter.4.cloned.1.call-done = bf16[128,512]{1,0:T(8,128)(2,1)} async-done(((bf16[256,512]{1,0:T(8,128)(2,1)}), bf16[128,512]{1,0:T(8,128)(2,1)}) %reduce-scatter.4.cloned.1.call-update) | async-done | bytes 131088
  995.6 4.6 collective-permute-done.20
  1003.5 3.5 collective-permute-start.22
  1007.0 4.0 collective-permute-done.22
  1011.0 4.4 collective-permute-start.23
  1015.4 5.9 collective-permute-done.23
  1021.3 7.6 collective-permute-start.24
  1028.9 9.8 collective-permute-done.24
  1038.7 12.0 %collective-permute-start.25 = (bf16[2,2,2,64,128]{4,3,0,2,1:T(8,128)(2,1)S(1)}, bf16[2,2,2,64,128]{4,3,0,2,1:T(8,128)(2,1)S(1)}, u32[]{:S(2)}, u32[]{:S(2)}) collective-permute-start(bf16[2,2,2,64,128]{4,3,0,2,1:T(8,128)(2,1)S(1)} %collective-permute-done.24), channel_id=1, source_target_pairs={{0,32},{32,0},{2,34},{34,2},{4,36},{36,4},{6,38},{38,6},{8,40},{40... | collective-permute-start | bytes 393224 | tf_op jit(solution)/shard_map/ppermute | solution.py:17
  1050.8 12.1 %collective-permute-done.25 = bf16[2,2,2,64,128]{4,3,0,2,1:T(8,128)(2,1)S(1)} collective-permute-done((bf16[2,2,2,64,128]{4,3,0,2,1:T(8,128)(2,1)S(1)}, bf16[2,2,2,64,128]{4,3,0,2,1:T(8,128)(2,1)S(1)}, u32[]{:S(2)}, u32[]{:S(2)}) %collective-permute-start.25) | collective-permute-done | bytes 131104 | tf_op jit(solution)/shard_map/ppermute | solution.py:17
  1065.3 4.4 collective-permute-done.26
  1069.7 4.0 collective-permute-start.27
  1073.7 4.4 collective-permute-done.27
  (284 shorter events, 172.9 us)
Async XLA Ops:
  6.5 218.0 %copy-start = (f32[512,256]{1,0:T(8,128)S(1)}, f32[512,256]{1,0:T(8,128)}, u32[]{:S(2)}) copy-start(f32[512,256]{1,0:T(8,128)} %param.13) | copy-start | bytes 1572868
  6.5 984.3 %reduce-scatter.4.cloned.1.call-start = ((), (), s32[]{:S(2)}) async-start(), calls=%async_computation.1 | async-start | bytes 393216
  6.5 199.4 %collective-permute-start.9 = (bf16[2,2,256,256]{3,2,1,0:T(8,128)(2,1)}, bf16[2,2,256,256]{3,2,1,0:T(8,128)(2,1)}, u32[]{:S(2)}, u32[]{:S(2)}) collective-permute-start(bf16[2,2,256,256]{3,2,1,0:T(8,128)(2,1)} %param.9), channel_id=1, source_target_pairs={{0,2},{2,4},{4,6},{6,8},{8,10},{10,12},{12,14},{14,16},{16,18},{18... | collective-permute-start | bytes 1572872 | tf_op jit(solution)/shard_map/ppermute | solution.py:22
  8.6 199.3 %collective-permute-start.15 = (bf16[2,2,256,256]{3,2,1,0:T(8,128)(2,1)}, bf16[2,2,256,256]{3,2,1,0:T(8,128)(2,1)}, u32[]{:S(2)}, u32[]{:S(2)}) collective-permute-start(bf16[2,2,256,256]{3,2,1,0:T(8,128)(2,1)} %param.9), channel_id=1, source_target_pairs={{0,254},{2,0},{4,2},{6,4},{8,6},{10,8},{12,10},{14,12},{16,14},{18... | collective-permute-start | bytes 1572872 | tf_op jit(solution)/shard_map/ppermute | solution.py:22
  19.4 178.6 %collective-permute-start.10 = (bf16[2,2,64,512]{3,2,1,0:T(8,128)(2,1)}, bf16[2,2,64,512]{3,2,1,0:T(8,128)(2,1)}, u32[]{:S(2)}, u32[]{:S(2)}) collective-permute-start(bf16[2,2,64,512]{3,2,1,0:T(8,128)(2,1)} %param.10), channel_id=1, source_target_pairs={{0,2},{2,4},{4,6},{6,8},{8,10},{10,12},{12,14},{14,16},{16,18},{18... | collective-permute-start | bytes 786440 | tf_op jit(solution)/shard_map/ppermute | solution.py:22
  21.3 178.8 %collective-permute-start.16 = (bf16[2,2,64,512]{3,2,1,0:T(8,128)(2,1)}, bf16[2,2,64,512]{3,2,1,0:T(8,128)(2,1)}, u32[]{:S(2)}, u32[]{:S(2)}) collective-permute-start(bf16[2,2,64,512]{3,2,1,0:T(8,128)(2,1)} %param.10), channel_id=1, source_target_pairs={{0,254},{2,0},{4,2},{6,4},{8,6},{10,8},{12,10},{14,12},{16,14},{18... | collective-permute-start | bytes 786440 | tf_op jit(solution)/shard_map/ppermute | solution.py:22
  28.1 41.6 %collective-permute-start = (bf16[2,2,2,64,256]{4,3,0,2,1:T(8,128)(2,1)S(1)}, bf16[2,2,2,64,256]{4,3,0,2,1:T(8,128)(2,1)S(1)}, u32[]{:S(2)}, u32[]{:S(2)}) collective-permute-start(bf16[2,2,2,64,256]{4,3,0,2,1:T(8,128)(2,1)S(1)} %bitcast.655), channel_id=1, source_target_pairs={{0,256},{256,0},{1,257},{257,1},{2,258},{258,2},{3,259},{259,3},{4... | collective-permute-start | bytes 786440 | tf_op jit(solution)/shard_map/ppermute | solution.py:17
  69.7 4.1 collective-permute-start.1
  73.9 10.7 collective-permute-start.2
  84.6 16.3 %collective-permute-start.3 = (bf16[2,2,2,64,256]{4,3,0,2,1:T(8,128)(2,1)S(1)}, bf16[2,2,2,64,256]{4,3,0,2,1:T(8,128)(2,1)S(1)}, u32[]{:S(2)}, u32[]{:S(2)}) collective-permute-start(bf16[2,2,2,64,256]{4,3,0,2,1:T(8,128)(2,1)S(1)} %collective-permute-done.2), channel_id=1, source_target_pairs={{0,8},{8,0},{2,10},{10,2},{4,12},{12,4},{6,14},{14,6},{16,24},{24,... | collective-permute-start | bytes 786440 | tf_op jit(solution)/shard_map/ppermute | solution.py:17
  100.8 27.1 %collective-permute-start.4 = (bf16[2,2,2,64,256]{4,3,0,2,1:T(8,128)(2,1)S(1)}, bf16[2,2,2,64,256]{4,3,0,2,1:T(8,128)(2,1)S(1)}, u32[]{:S(2)}, u32[]{:S(2)}) collective-permute-start(bf16[2,2,2,64,256]{4,3,0,2,1:T(8,128)(2,1)S(1)} %collective-permute-done.3), channel_id=1, source_target_pairs={{0,16},{16,0},{2,18},{18,2},{4,20},{20,4},{6,22},{22,6},{8,24},{24... | collective-permute-start | bytes 786440 | tf_op jit(solution)/shard_map/ppermute | solution.py:17
  128.0 31.6 %collective-permute-start.5 = (bf16[2,2,2,64,256]{4,3,0,2,1:T(8,128)(2,1)S(1)}, bf16[2,2,2,64,256]{4,3,0,2,1:T(8,128)(2,1)S(1)}, u32[]{:S(2)}, u32[]{:S(2)}) collective-permute-start(bf16[2,2,2,64,256]{4,3,0,2,1:T(8,128)(2,1)S(1)} %collective-permute-done.4), channel_id=1, source_target_pairs={{0,32},{32,0},{2,34},{34,2},{4,36},{36,4},{6,38},{38,6},{8,40},{40... | collective-permute-start | bytes 786440 | tf_op jit(solution)/shard_map/ppermute | solution.py:17
  159.6 10.2 collective-permute-start.6
  169.8 43.8 %collective-permute-start.7 = (bf16[2,2,2,64,256]{4,3,0,2,1:T(8,128)(2,1)}, bf16[2,2,2,64,256]{4,3,0,2,1:T(8,128)(2,1)}, u32[]{:S(2)}, u32[]{:S(2)}) collective-permute-start(bf16[2,2,2,64,256]{4,3,0,2,1:T(8,128)(2,1)} %collective-permute-done.6), channel_id=1, source_target_pairs={{0,128},{128,0},{2,130},{130,2},{4,132},{132,4},{6,134},{134,6},{8... | collective-permute-start | bytes 786440 | tf_op jit(solution)/shard_map/ppermute | solution.py:17
  198.1 654.0 %collective-permute-start.13 = (bf16[2,2,64,512]{3,2,1,0:T(8,128)(2,1)}, bf16[2,2,64,512]{3,2,1,0:T(8,128)(2,1)}, u32[]{:S(2)}, u32[]{:S(2)}) collective-permute-start(bf16[2,2,64,512]{3,2,1,0:T(8,128)(2,1)} %collective-permute-done.10), channel_id=1, source_target_pairs={{0,2},{2,4},{4,6},{6,8},{8,10},{10,12},{12,14},{14,16},{16,18},{18... | collective-permute-start | bytes 786440 | tf_op jit(solution)/shard_map/ppermute | solution.py:22
  200.1 664.4 %collective-permute-start.19 = (bf16[2,2,64,512]{3,2,1,0:T(8,128)(2,1)}, bf16[2,2,64,512]{3,2,1,0:T(8,128)(2,1)}, u32[]{:S(2)}, u32[]{:S(2)}) collective-permute-start(bf16[2,2,64,512]{3,2,1,0:T(8,128)(2,1)} %collective-permute-done.16), channel_id=1, source_target_pairs={{0,254},{2,0},{4,2},{6,4},{8,6},{10,8},{12,10},{14,12},{16,14},{18... | collective-permute-start | bytes 786440 | tf_op jit(solution)/shard_map/ppermute | solution.py:22
  205.9 636.3 %collective-permute-start.12 = (bf16[2,2,256,256]{3,2,1,0:T(8,128)(2,1)}, bf16[2,2,256,256]{3,2,1,0:T(8,128)(2,1)}, u32[]{:S(2)}, u32[]{:S(2)}) collective-permute-start(bf16[2,2,256,256]{3,2,1,0:T(8,128)(2,1)} %collective-permute-done.9), channel_id=1, source_target_pairs={{0,2},{2,4},{4,6},{6,8},{8,10},{10,12},{12,14},{14,16},{16,18},{18... | collective-permute-start | bytes 1572872 | tf_op jit(solution)/shard_map/ppermute | solution.py:22
  207.9 652.0 %collective-permute-start.18 = (bf16[2,2,256,256]{3,2,1,0:T(8,128)(2,1)}, bf16[2,2,256,256]{3,2,1,0:T(8,128)(2,1)}, u32[]{:S(2)}, u32[]{:S(2)}) collective-permute-start(bf16[2,2,256,256]{3,2,1,0:T(8,128)(2,1)} %collective-permute-done.15), channel_id=1, source_target_pairs={{0,254},{2,0},{4,2},{6,4},{8,6},{10,8},{12,10},{14,12},{16,14},{18... | collective-permute-start | bytes 1572872 | tf_op jit(solution)/shard_map/ppermute | solution.py:22
  217.9 594.7 %collective-permute-start.8 = (bf16[2,2,2,64,256]{4,3,0,2,1:T(8,128)(2,1)}, bf16[2,2,2,64,256]{4,3,0,2,1:T(8,128)(2,1)}, u32[]{:S(2)}, u32[]{:S(2)}) collective-permute-start(bf16[2,2,2,64,256]{4,3,0,2,1:T(8,128)(2,1)} %fusion.89), channel_id=1, source_target_pairs={{0,2},{2,4},{4,6},{6,8},{8,10},{10,12},{12,14},{14,16},{16,18},{18... | collective-permute-start | bytes 786440 | tf_op jit(solution)/shard_map/ppermute | solution.py:22
  225.0 584.7 %copy-start.46 = (bf16[2,2,64,256]{3,2,1,0:T(8,128)(2,1)S(1)}, bf16[2,2,64,256]{3,2,1,0:T(8,128)(2,1)}, u32[]{:S(2)}) copy-start(bf16[2,2,64,256]{3,2,1,0:T(8,128)(2,1)} %get-tuple-element.68) | copy-start | bytes 393220
  812.6 14.6 %collective-permute-start.14 = (bf16[2,2,2,64,256]{4,3,0,2,1:T(8,128)(2,1)}, bf16[2,2,2,64,256]{4,3,0,2,1:T(8,128)(2,1)S(1)}, u32[]{:S(2)}, u32[]{:S(2)}) collective-permute-start(bf16[2,2,2,64,256]{4,3,0,2,1:T(8,128)(2,1)} %fusion.89), channel_id=1, source_target_pairs={{0,254},{2,0},{4,2},{6,4},{8,6},{10,8},{12,10},{14,12},{16,14},{18... | collective-permute-start | bytes 786440 | tf_op jit(solution)/shard_map/ppermute | solution.py:22
  827.2 20.3 %collective-permute-start.11 = (bf16[2,2,2,64,256]{4,3,0,2,1:T(8,128)(2,1)}, bf16[2,2,2,64,256]{4,3,0,2,1:T(8,128)(2,1)S(1)}, u32[]{:S(2)}, u32[]{:S(2)}) collective-permute-start(bf16[2,2,2,64,256]{4,3,0,2,1:T(8,128)(2,1)} %collective-permute-done.8), channel_id=1, source_target_pairs={{0,2},{2,4},{4,6},{6,8},{8,10},{10,12},{12,14},{14,16},{16,18},{18... | collective-permute-start | bytes 786440 | tf_op jit(solution)/shard_map/ppermute | solution.py:22
  842.2 17.7 %collective-permute-start.17 = (bf16[2,2,2,64,256]{4,3,0,2,1:T(8,128)(2,1)S(1)}, bf16[2,2,2,64,256]{4,3,0,2,1:T(8,128)(2,1)S(1)}, u32[]{:S(2)}, u32[]{:S(2)}) collective-permute-start(bf16[2,2,2,64,256]{4,3,0,2,1:T(8,128)(2,1)S(1)} %collective-permute-done.14), channel_id=1, source_target_pairs={{0,254},{2,0},{4,2},{6,4},{8,6},{10,8},{12,10},{14,12},{16,14},{18... | collective-permute-start | bytes 786440 | tf_op jit(solution)/shard_map/ppermute | solution.py:22
  896.9 182.0 %copy-start.1 = (f32[512,256]{1,0:T(8,128)S(1)}, f32[512,256]{1,0:T(8,128)}, u32[]{:S(2)}) copy-start(f32[512,256]{1,0:T(8,128)} %param.13) | copy-start | bytes 1572868
  993.1 7.1 collective-permute-start.20
  1000.3 3.2 collective-permute-start.21
  1003.5 7.4 collective-permute-start.22
  1011.0 10.3 collective-permute-start.23
  1021.3 17.5 %collective-permute-start.24 = (bf16[2,2,2,64,128]{4,3,0,2,1:T(8,128)(2,1)S(1)}, bf16[2,2,2,64,128]{4,3,0,2,1:T(8,128)(2,1)S(1)}, u32[]{:S(2)}, u32[]{:S(2)}) collective-permute-start(bf16[2,2,2,64,128]{4,3,0,2,1:T(8,128)(2,1)S(1)} %collective-permute-done.23), channel_id=1, source_target_pairs={{0,16},{16,0},{2,18},{18,2},{4,20},{20,4},{6,22},{22,6},{8,24},{24... | collective-permute-start | bytes 393224 | tf_op jit(solution)/shard_map/ppermute | solution.py:17
  1038.7 24.1 %collective-permute-start.25 = (bf16[2,2,2,64,128]{4,3,0,2,1:T(8,128)(2,1)S(1)}, bf16[2,2,2,64,128]{4,3,0,2,1:T(8,128)(2,1)S(1)}, u32[]{:S(2)}, u32[]{:S(2)}) collective-permute-start(bf16[2,2,2,64,128]{4,3,0,2,1:T(8,128)(2,1)S(1)} %collective-permute-done.24), channel_id=1, source_target_pairs={{0,32},{32,0},{2,34},{34,2},{4,36},{36,4},{6,38},{38,6},{8,40},{40... | collective-permute-start | bytes 393224 | tf_op jit(solution)/shard_map/ppermute | solution.py:17
  1062.9 6.8 collective-permute-start.26
  1069.7 8.4 collective-permute-start.27
  (58 other events, 577.1 us)
Sparse Core Ops, SparseCore 0:
  898.5 92.2 reduce-scatter.3
where the time goes:
time: 1100 us; the launch traced here: 1090 us
  blocking collectives  583 us (53%)
  waiting for transfers between devices  201 us (18%)
  starting transfers between devices  120 us (11%)
  matrix products  76.3 us (7%)
  other arithmetic  56 us (5%)
  local copies, waits for them, and re-layouts  35.4 us (3%)
  between operations  15.1 us (1%)
    psum x1, blocking collectives, per_device(): spread = lax.psum(spread, ('ka', 'isdf'))  583 us
    ppermute x16, waiting for transfers between devices, swapped(): return lax.ppermute(block, axis, route)  108 us
    unnamed x2, waiting for transfers between devices  92.5 us
    ppermute x16, starting transfers between devices, swapped(): return lax.ppermute(block, axis, route)  71.9 us
    dot_general x48, matrix products, single(): jnp.einsum(pattern, first, second, preferred_element_type=jnp.float32)  53.4 us
    ppermute x12, starting transfers between devices, shifted(): lax.ppermute(value, axis, [(i, (i + by) % size) for i in range(size)])  47.7 us
    mul x10, other arithmetic, accumulate(): screen_real * visit_real - screen_imag * visit_imag  23 us
    dot_general x10, matrix products, accumulate(): jnp.einsum('kw,wrmn->rkmn', selector[:, visitor], screened, preferred_ele...  22.4 us
  transfers between devices with their start and end apart: 29, of which 14 were waited for; matrix products, arithmetic and copies ran while one was open for 12% of the time, Pallas kernels for 0%

commit v1 on v0

--- a/solution.py
+++ b/solution.py
@@ -101,7 +101,7 @@
     )
     density = jnp.stack([rho_real, rho_imag], axis=1)
     spread = jnp.einsum("nm,brm->brn", coulomb, density, precision=HIGHEST)
-    spread = lax.psum(spread, ("ka", "isdf"))
+    spread = lax.psum(lax.psum(spread, "isdf"), "ka")
     potential = lax.dynamic_slice_in_dim(spread, isdf_index * mu_count, mu_count, 2)
     class_ids = jnp.arange(screened.shape[0], dtype=jnp.int32)
 

time: 1100 us -> 699 us (0.64)
  blocking collectives: 583 us -> 221 us
  waiting for transfers between devices: 201 us -> 165 us
    psum x1 -> x2, blocking collectives: 583 us -> 221 us  [per_device(): spread = lax.psum(lax.psum(spread, 'isdf'), 'ka')]
    unnamed x2, waiting for transfers between devices: 92.5 us -> 56.5 us
  transfers between devices with their start and end apart: 29 -> 29, of which waited for: 14 -> 14; matrix products, arithmetic and copies ran while one was open for 12% -> 19% of each run, Pallas kernels for 0% -> 0%
where the time goes in v1:
time: 699 us; the launch traced here: 689 us
  blocking collectives  221 us (32%)
  waiting for transfers between devices  165 us (24%)
  starting transfers between devices  120 us (17%)
  matrix products  76.2 us (11%)
  other arithmetic  55.9 us (8%)
  local copies, waits for them, and re-layouts  35.4 us (5%)
  between operations  15.1 us (2%)
    psum x2, blocking collectives, per_device(): spread = lax.psum(lax.psum(spread, 'isdf'), 'ka')  221 us
    ppermute x16, waiting for transfers between devices, swapped(): return lax.ppermute(block, axis, route)  108 us
    ppermute x16, starting transfers between devices, swapped(): return lax.ppermute(block, axis, route)  71.8 us
    unnamed x2, waiting for transfers between devices  56.5 us
    dot_general x48, matrix products, single(): jnp.einsum(pattern, first, second, preferred_element_type=jnp.float32)  53.4 us
    ppermute x12, starting transfers between devices, shifted(): lax.ppermute(value, axis, [(i, (i + by) % size) for i in range(size)])  47.7 us
    mul x10, other arithmetic, accumulate(): screen_real * visit_real - screen_imag * visit_imag  22.9 us
    dot_general x10, matrix products, accumulate(): jnp.einsum('kw,wrmn->rkmn', selector[:, visitor], screened, preferred_ele...  22.4 us
  transfers between devices with their start and end apart: 29, of which 14 were waited for; matrix products, arithmetic and copies ran while one was open for 19% of the time, Pallas kernels for 0%

profile of v1, /device:TPU:2, one launch (start us, length us, event | category | flops | bytes accessed | tf_op | source)
XLA Modules:
  0.0 688.6 jit_solution(6555879929286694897)
XLA Ops:
  8.6 10.8 %collective-permute-start.15 = (bf16[2,2,256,256]{3,2,1,0:T(8,128)(2,1)}, bf16[2,2,256,256]{3,2,1,0:T(8,128)(2,1)}, u32[]{:S(2)}, u32[]{:S(2)}) collective-permute-start(bf16[2,2,256,256]{3,2,1,0:T(8,128)(2,1)} %param.9), channel_id=1, source_target_pairs={{0,254},{2,0},{4,2},{6,4},{8,6},{10,8},{12,10},{14,12},{16,14},{18... | collective-permute-start | bytes 1572872 | tf_op jit(solution)/shard_map/ppermute | solution.py:22
  21.3 5.8 collective-permute-start.16
  28.1 3.5 collective-permute-start
  32.8 3.2 copy.48
  66.2 3.5 fusion.75
  78.0 6.5 collective-permute-done.2
  88.5 12.3 %collective-permute-done.3 = bf16[2,2,2,64,256]{4,3,0,2,1:T(8,128)(2,1)S(1)} collective-permute-done((bf16[2,2,2,64,256]{4,3,0,2,1:T(8,128)(2,1)S(1)}, bf16[2,2,2,64,256]{4,3,0,2,1:T(8,128)(2,1)S(1)}, u32[]{:S(2)}, u32[]{:S(2)}) %collective-permute-start.3) | collective-permute-done | bytes 262176 | tf_op jit(solution)/shard_map/ppermute | solution.py:17
  105.3 22.7 %collective-permute-done.4 = bf16[2,2,2,64,256]{4,3,0,2,1:T(8,128)(2,1)S(1)} collective-permute-done((bf16[2,2,2,64,256]{4,3,0,2,1:T(8,128)(2,1)S(1)}, bf16[2,2,2,64,256]{4,3,0,2,1:T(8,128)(2,1)S(1)}, u32[]{:S(2)}, u32[]{:S(2)}) %collective-permute-start.4) | collective-permute-done | bytes 262176 | tf_op jit(solution)/shard_map/ppermute | solution.py:17
  128.0 14.7 %collective-permute-start.5 = (bf16[2,2,2,64,256]{4,3,0,2,1:T(8,128)(2,1)S(1)}, bf16[2,2,2,64,256]{4,3,0,2,1:T(8,128)(2,1)S(1)}, u32[]{:S(2)}, u32[]{:S(2)}) collective-permute-start(bf16[2,2,2,64,256]{4,3,0,2,1:T(8,128)(2,1)S(1)} %collective-permute-done.4), channel_id=1, source_target_pairs={{0,32},{32,0},{2,34},{34,2},{4,36},{36,4},{6,38},{38,6},{8,40},{40... | collective-permute-start | bytes 786440 | tf_op jit(solution)/shard_map/ppermute | solution.py:17
  144.7 14.9 %collective-permute-done.5 = bf16[2,2,2,64,256]{4,3,0,2,1:T(8,128)(2,1)S(1)} collective-permute-done((bf16[2,2,2,64,256]{4,3,0,2,1:T(8,128)(2,1)S(1)}, bf16[2,2,2,64,256]{4,3,0,2,1:T(8,128)(2,1)S(1)}, u32[]{:S(2)}, u32[]{:S(2)}) %collective-permute-start.5) | collective-permute-done | bytes 262176 | tf_op jit(solution)/shard_map/ppermute | solution.py:17
  164.3 5.4 collective-permute-done.6
  169.8 4.2 collective-permute-start.7
  200.1 5.8 collective-permute-start.19
  207.8 5.8 collective-permute-start.18
  225.0 6.6 psum.14
  231.6 214.8 %psum.15 = f32[2,2,512]{2,1,0:T(2,128)S(1)} all-reduce(f32[2,2,512]{2,1,0:T(2,128)S(1)} %psum.14), channel_id=1, replica_groups=mesh['pm'=2,'ka'=128,'isdf'=2] {'ka'}, use_global_device_ids=true, to_apply=%region_1.2 | all-reduce | flops 2048 | bytes 16384 | tf_op jit(solution)/shard_map/psum | solution.py:104
  480.6 5.2 collective-permute-start.17
  513.6 9.2 %add_convert_fusion = bf16[2,2,256,512]{3,2,0,1:T(8,128)(2,1)S(1)} fusion(f32[2,256,512]{2,1,0:T(8,128)} %get-tuple-element.46, f32[2,256,512]{2,1,0:T(8,128)S(1)} %copy-done.19, f32[2,256,512]{2,1,0:T(8,128)} %get-tuple-element.71, f32[2,256,512]{2,1,0:T(8,128)S(1)} %copy-done.18, f32[2,256,512]{2,1,0:T(8,128)} %get-tuple-element.45, ...), kind=kLoop, calls=%fused_computation | loop fusion | flops 20971520 | bytes 42991616 | tf_op jit(solution)/shard_map/convert_element_type | solution.py:156
  522.8 9.5 %add_convert_fusion.1 = bf16[2,2,256,512]{3,2,0,1:T(8,128)(2,1)S(1)} fusion(f32[2,256,512]{2,1,0:T(8,128)} %get-tuple-element.46, f32[2,256,512]{2,1,0:T(8,128)S(1)} %copy-done.19, f32[2,256,512]{2,1,0:T(8,128)} %get-tuple-element.71, f32[2,256,512]{2,1,0:T(8,128)S(1)} %copy-done.18, f32[2,256,512]{2,1,0:T(8,128)} %get-tuple-element.45, ...), kind=kLoop, calls=%fused_computation.1 | loop fusion | flops 20971520 | bytes 42991616 | tf_op jit(solution)/shard_map/convert_element_type | solution.py:155
  536.7 56.5 %reduce-scatter.4.cloned.1.call-done = bf16[128,512]{1,0:T(8,128)(2,1)} async-done(((bf16[256,512]{1,0:T(8,128)(2,1)}), bf16[128,512]{1,0:T(8,128)(2,1)}) %reduce-scatter.4.cloned.1.call-update) | async-done | bytes 131088
  598.0 4.6 collective-permute-done.20
  605.9 3.4 collective-permute-start.22
  609.4 4.0 collective-permute-done.22
  613.4 4.4 collective-permute-start.23
  617.8 5.9 collective-permute-done.23
  623.7 7.6 %collective-permute-start.24 = (bf16[2,2,2,64,128]{4,3,0,2,1:T(8,128)(2,1)S(1)}, bf16[2,2,2,64,128]{4,3,0,2,1:T(8,128)(2,1)S(1)}, u32[]{:S(2)}, u32[]{:S(2)}) collective-permute-start(bf16[2,2,2,64,128]{4,3,0,2,1:T(8,128)(2,1)S(1)} %collective-permute-done.23), channel_id=1, source_target_pairs={{0,16},{16,0},{2,18},{18,2},{4,20},{20,4},{6,22},{22,6},{8,24},{24... | collective-permute-start | bytes 393224 | tf_op jit(solution)/shard_map/ppermute | solution.py:17
  631.3 9.9 %collective-permute-done.24 = bf16[2,2,2,64,128]{4,3,0,2,1:T(8,128)(2,1)S(1)} collective-permute-done((bf16[2,2,2,64,128]{4,3,0,2,1:T(8,128)(2,1)S(1)}, bf16[2,2,2,64,128]{4,3,0,2,1:T(8,128)(2,1)S(1)}, u32[]{:S(2)}, u32[]{:S(2)}) %collective-permute-start.24) | collective-permute-done | bytes 131104 | tf_op jit(solution)/shard_map/ppermute | solution.py:17
  641.2 12.0 %collective-permute-start.25 = (bf16[2,2,2,64,128]{4,3,0,2,1:T(8,128)(2,1)S(1)}, bf16[2,2,2,64,128]{4,3,0,2,1:T(8,128)(2,1)S(1)}, u32[]{:S(2)}, u32[]{:S(2)}) collective-permute-start(bf16[2,2,2,64,128]{4,3,0,2,1:T(8,128)(2,1)S(1)} %collective-permute-done.24), channel_id=1, source_target_pairs={{0,32},{32,0},{2,34},{34,2},{4,36},{36,4},{6,38},{38,6},{8,40},{40... | collective-permute-start | bytes 393224 | tf_op jit(solution)/shard_map/ppermute | solution.py:17
  653.2 12.1 %collective-permute-done.25 = bf16[2,2,2,64,128]{4,3,0,2,1:T(8,128)(2,1)S(1)} collective-permute-done((bf16[2,2,2,64,128]{4,3,0,2,1:T(8,128)(2,1)S(1)}, bf16[2,2,2,64,128]{4,3,0,2,1:T(8,128)(2,1)S(1)}, u32[]{:S(2)}, u32[]{:S(2)}) %collective-permute-start.25) | collective-permute-done | bytes 131104 | tf_op jit(solution)/shard_map/ppermute | solution.py:17
  667.6 4.5 collective-permute-done.26
  672.1 4.0 collective-permute-start.27
  676.1 4.4 collective-permute-done.27
  (285 shorter events, 175.7 us)
Async XLA Ops:
  6.5 217.9 %copy-start = (f32[512,256]{1,0:T(8,128)S(1)}, f32[512,256]{1,0:T(8,128)}, u32[]{:S(2)}) copy-start(f32[512,256]{1,0:T(8,128)} %param.13) | copy-start | bytes 1572868
  6.5 586.7 %reduce-scatter.4.cloned.1.call-start = ((), (), s32[]{:S(2)}) async-start(), calls=%async_computation.1 | async-start | bytes 393216
  6.5 199.3 %collective-permute-start.9 = (bf16[2,2,256,256]{3,2,1,0:T(8,128)(2,1)}, bf16[2,2,256,256]{3,2,1,0:T(8,128)(2,1)}, u32[]{:S(2)}, u32[]{:S(2)}) collective-permute-start(bf16[2,2,256,256]{3,2,1,0:T(8,128)(2,1)} %param.9), channel_id=1, source_target_pairs={{0,2},{2,4},{4,6},{6,8},{8,10},{10,12},{12,14},{14,16},{16,18},{18... | collective-permute-start | bytes 1572872 | tf_op jit(solution)/shard_map/ppermute | solution.py:22
  8.6 199.2 %collective-permute-start.15 = (bf16[2,2,256,256]{3,2,1,0:T(8,128)(2,1)}, bf16[2,2,256,256]{3,2,1,0:T(8,128)(2,1)}, u32[]{:S(2)}, u32[]{:S(2)}) collective-permute-start(bf16[2,2,256,256]{3,2,1,0:T(8,128)(2,1)} %param.9), channel_id=1, source_target_pairs={{0,254},{2,0},{4,2},{6,4},{8,6},{10,8},{12,10},{14,12},{16,14},{18... | collective-permute-start | bytes 1572872 | tf_op jit(solution)/shard_map/ppermute | solution.py:22
  19.4 178.6 %collective-permute-start.10 = (bf16[2,2,64,512]{3,2,1,0:T(8,128)(2,1)}, bf16[2,2,64,512]{3,2,1,0:T(8,128)(2,1)}, u32[]{:S(2)}, u32[]{:S(2)}) collective-permute-start(bf16[2,2,64,512]{3,2,1,0:T(8,128)(2,1)} %param.10), channel_id=1, source_target_pairs={{0,2},{2,4},{4,6},{6,8},{8,10},{10,12},{12,14},{14,16},{16,18},{18... | collective-permute-start | bytes 786440 | tf_op jit(solution)/shard_map/ppermute | solution.py:22
  21.3 178.7 %collective-permute-start.16 = (bf16[2,2,64,512]{3,2,1,0:T(8,128)(2,1)}, bf16[2,2,64,512]{3,2,1,0:T(8,128)(2,1)}, u32[]{:S(2)}, u32[]{:S(2)}) collective-permute-start(bf16[2,2,64,512]{3,2,1,0:T(8,128)(2,1)} %param.10), channel_id=1, source_target_pairs={{0,254},{2,0},{4,2},{6,4},{8,6},{10,8},{12,10},{14,12},{16,14},{18... | collective-permute-start | bytes 786440 | tf_op jit(solution)/shard_map/ppermute | solution.py:22
  28.1 41.6 %collective-permute-start = (bf16[2,2,2,64,256]{4,3,0,2,1:T(8,128)(2,1)S(1)}, bf16[2,2,2,64,256]{4,3,0,2,1:T(8,128)(2,1)S(1)}, u32[]{:S(2)}, u32[]{:S(2)}) collective-permute-start(bf16[2,2,2,64,256]{4,3,0,2,1:T(8,128)(2,1)S(1)} %bitcast.655), channel_id=1, source_target_pairs={{0,256},{256,0},{1,257},{257,1},{2,258},{258,2},{3,259},{259,3},{4... | collective-permute-start | bytes 786440 | tf_op jit(solution)/shard_map/ppermute | solution.py:17
  69.7 4.1 collective-permute-start.1
  73.8 10.7 %collective-permute-start.2 = (bf16[2,2,2,64,256]{4,3,0,2,1:T(8,128)(2,1)S(1)}, bf16[2,2,2,64,256]{4,3,0,2,1:T(8,128)(2,1)S(1)}, u32[]{:S(2)}, u32[]{:S(2)}) collective-permute-start(bf16[2,2,2,64,256]{4,3,0,2,1:T(8,128)(2,1)S(1)} %collective-permute-done.1), channel_id=1, source_target_pairs={{0,4},{4,0},{2,6},{6,2},{8,12},{12,8},{10,14},{14,10},{16,20},{20,... | collective-permute-start | bytes 786440 | tf_op jit(solution)/shard_map/ppermute | solution.py:17
  84.6 16.3 %collective-permute-start.3 = (bf16[2,2,2,64,256]{4,3,0,2,1:T(8,128)(2,1)S(1)}, bf16[2,2,2,64,256]{4,3,0,2,1:T(8,128)(2,1)S(1)}, u32[]{:S(2)}, u32[]{:S(2)}) collective-permute-start(bf16[2,2,2,64,256]{4,3,0,2,1:T(8,128)(2,1)S(1)} %collective-permute-done.2), channel_id=1, source_target_pairs={{0,8},{8,0},{2,10},{10,2},{4,12},{12,4},{6,14},{14,6},{16,24},{24,... | collective-permute-start | bytes 786440 | tf_op jit(solution)/shard_map/ppermute | solution.py:17
  100.8 27.1 %collective-permute-start.4 = (bf16[2,2,2,64,256]{4,3,0,2,1:T(8,128)(2,1)S(1)}, bf16[2,2,2,64,256]{4,3,0,2,1:T(8,128)(2,1)S(1)}, u32[]{:S(2)}, u32[]{:S(2)}) collective-permute-start(bf16[2,2,2,64,256]{4,3,0,2,1:T(8,128)(2,1)S(1)} %collective-permute-done.3), channel_id=1, source_target_pairs={{0,16},{16,0},{2,18},{18,2},{4,20},{20,4},{6,22},{22,6},{8,24},{24... | collective-permute-start | bytes 786440 | tf_op jit(solution)/shard_map/ppermute | solution.py:17
  128.0 31.6 %collective-permute-start.5 = (bf16[2,2,2,64,256]{4,3,0,2,1:T(8,128)(2,1)S(1)}, bf16[2,2,2,64,256]{4,3,0,2,1:T(8,128)(2,1)S(1)}, u32[]{:S(2)}, u32[]{:S(2)}) collective-permute-start(bf16[2,2,2,64,256]{4,3,0,2,1:T(8,128)(2,1)S(1)} %collective-permute-done.4), channel_id=1, source_target_pairs={{0,32},{32,0},{2,34},{34,2},{4,36},{36,4},{6,38},{38,6},{8,40},{40... | collective-permute-start | bytes 786440 | tf_op jit(solution)/shard_map/ppermute | solution.py:17
  159.6 10.2 %collective-permute-start.6 = (bf16[2,2,2,64,256]{4,3,0,2,1:T(8,128)(2,1)S(1)}, bf16[2,2,2,64,256]{4,3,0,2,1:T(8,128)(2,1)}, u32[]{:S(2)}, u32[]{:S(2)}) collective-permute-start(bf16[2,2,2,64,256]{4,3,0,2,1:T(8,128)(2,1)S(1)} %collective-permute-done.5), channel_id=1, source_target_pairs={{0,64},{64,0},{2,66},{66,2},{4,68},{68,4},{6,70},{70,6},{8,72},{72... | collective-permute-start | bytes 786440 | tf_op jit(solution)/shard_map/ppermute | solution.py:17
  169.8 43.8 %collective-permute-start.7 = (bf16[2,2,2,64,256]{4,3,0,2,1:T(8,128)(2,1)}, bf16[2,2,2,64,256]{4,3,0,2,1:T(8,128)(2,1)}, u32[]{:S(2)}, u32[]{:S(2)}) collective-permute-start(bf16[2,2,2,64,256]{4,3,0,2,1:T(8,128)(2,1)} %collective-permute-done.6), channel_id=1, source_target_pairs={{0,128},{128,0},{2,130},{130,2},{4,132},{132,4},{6,134},{134,6},{8... | collective-permute-start | bytes 786440 | tf_op jit(solution)/shard_map/ppermute | solution.py:17
  198.0 292.4 %collective-permute-start.13 = (bf16[2,2,64,512]{3,2,1,0:T(8,128)(2,1)}, bf16[2,2,64,512]{3,2,1,0:T(8,128)(2,1)}, u32[]{:S(2)}, u32[]{:S(2)}) collective-permute-start(bf16[2,2,64,512]{3,2,1,0:T(8,128)(2,1)} %collective-permute-done.10), channel_id=1, source_target_pairs={{0,2},{2,4},{4,6},{6,8},{8,10},{10,12},{12,14},{14,16},{16,18},{18... | collective-permute-start | bytes 786440 | tf_op jit(solution)/shard_map/ppermute | solution.py:22
  200.1 302.8 %collective-permute-start.19 = (bf16[2,2,64,512]{3,2,1,0:T(8,128)(2,1)}, bf16[2,2,64,512]{3,2,1,0:T(8,128)(2,1)}, u32[]{:S(2)}, u32[]{:S(2)}) collective-permute-start(bf16[2,2,64,512]{3,2,1,0:T(8,128)(2,1)} %collective-permute-done.16), channel_id=1, source_target_pairs={{0,254},{2,0},{4,2},{6,4},{8,6},{10,8},{12,10},{14,12},{16,14},{18... | collective-permute-start | bytes 786440 | tf_op jit(solution)/shard_map/ppermute | solution.py:22
  205.9 274.8 %collective-permute-start.12 = (bf16[2,2,256,256]{3,2,1,0:T(8,128)(2,1)}, bf16[2,2,256,256]{3,2,1,0:T(8,128)(2,1)}, u32[]{:S(2)}, u32[]{:S(2)}) collective-permute-start(bf16[2,2,256,256]{3,2,1,0:T(8,128)(2,1)} %collective-permute-done.9), channel_id=1, source_target_pairs={{0,2},{2,4},{4,6},{6,8},{8,10},{10,12},{12,14},{14,16},{16,18},{18... | collective-permute-start | bytes 1572872 | tf_op jit(solution)/shard_map/ppermute | solution.py:22
  207.8 290.4 %collective-permute-start.18 = (bf16[2,2,256,256]{3,2,1,0:T(8,128)(2,1)}, bf16[2,2,256,256]{3,2,1,0:T(8,128)(2,1)}, u32[]{:S(2)}, u32[]{:S(2)}) collective-permute-start(bf16[2,2,256,256]{3,2,1,0:T(8,128)(2,1)} %collective-permute-done.15), channel_id=1, source_target_pairs={{0,254},{2,0},{4,2},{6,4},{8,6},{10,8},{12,10},{14,12},{16,14},{18... | collective-permute-start | bytes 1572872 | tf_op jit(solution)/shard_map/ppermute | solution.py:22
  217.8 233.1 %collective-permute-start.8 = (bf16[2,2,2,64,256]{4,3,0,2,1:T(8,128)(2,1)}, bf16[2,2,2,64,256]{4,3,0,2,1:T(8,128)(2,1)}, u32[]{:S(2)}, u32[]{:S(2)}) collective-permute-start(bf16[2,2,2,64,256]{4,3,0,2,1:T(8,128)(2,1)} %fusion.89), channel_id=1, source_target_pairs={{0,2},{2,4},{4,6},{6,8},{8,10},{10,12},{12,14},{14,16},{16,18},{18... | collective-permute-start | bytes 786440 | tf_op jit(solution)/shard_map/ppermute | solution.py:22
  225.0 223.1 %copy-start.46 = (bf16[2,2,64,256]{3,2,1,0:T(8,128)(2,1)S(1)}, bf16[2,2,64,256]{3,2,1,0:T(8,128)(2,1)}, u32[]{:S(2)}) copy-start(bf16[2,2,64,256]{3,2,1,0:T(8,128)(2,1)} %get-tuple-element.68) | copy-start | bytes 393220
  450.9 14.6 %collective-permute-start.14 = (bf16[2,2,2,64,256]{4,3,0,2,1:T(8,128)(2,1)}, bf16[2,2,2,64,256]{4,3,0,2,1:T(8,128)(2,1)S(1)}, u32[]{:S(2)}, u32[]{:S(2)}) collective-permute-start(bf16[2,2,2,64,256]{4,3,0,2,1:T(8,128)(2,1)} %fusion.89), channel_id=1, source_target_pairs={{0,254},{2,0},{4,2},{6,4},{8,6},{10,8},{12,10},{14,12},{16,14},{18... | collective-permute-start | bytes 786440 | tf_op jit(solution)/shard_map/ppermute | solution.py:22
  465.6 20.3 %collective-permute-start.11 = (bf16[2,2,2,64,256]{4,3,0,2,1:T(8,128)(2,1)}, bf16[2,2,2,64,256]{4,3,0,2,1:T(8,128)(2,1)S(1)}, u32[]{:S(2)}, u32[]{:S(2)}) collective-permute-start(bf16[2,2,2,64,256]{4,3,0,2,1:T(8,128)(2,1)} %collective-permute-done.8), channel_id=1, source_target_pairs={{0,2},{2,4},{4,6},{6,8},{8,10},{10,12},{12,14},{14,16},{16,18},{18... | collective-permute-start | bytes 786440 | tf_op jit(solution)/shard_map/ppermute | solution.py:22
  480.6 17.6 %collective-permute-start.17 = (bf16[2,2,2,64,256]{4,3,0,2,1:T(8,128)(2,1)S(1)}, bf16[2,2,2,64,256]{4,3,0,2,1:T(8,128)(2,1)S(1)}, u32[]{:S(2)}, u32[]{:S(2)}) collective-permute-start(bf16[2,2,2,64,256]{4,3,0,2,1:T(8,128)(2,1)S(1)} %collective-permute-done.14), channel_id=1, source_target_pairs={{0,254},{2,0},{4,2},{6,4},{8,6},{10,8},{12,10},{14,12},{16,14},{18... | collective-permute-start | bytes 786440 | tf_op jit(solution)/shard_map/ppermute | solution.py:22
  535.2 146.1 %copy-start.1 = (f32[512,256]{1,0:T(8,128)S(1)}, f32[512,256]{1,0:T(8,128)}, u32[]{:S(2)}) copy-start(f32[512,256]{1,0:T(8,128)} %param.13) | copy-start | bytes 1572868
  595.5 7.1 %collective-permute-start.20 = (bf16[2,2,2,64,128]{4,3,0,2,1:T(8,128)(2,1)S(1)}, bf16[2,2,2,64,128]{4,3,0,2,1:T(8,128)(2,1)S(1)}, u32[]{:S(2)}, u32[]{:S(2)}) collective-permute-start(bf16[2,2,2,64,128]{4,3,0,2,1:T(8,128)(2,1)S(1)} %add_convert_fusion.7), channel_id=1, source_target_pairs={{0,256},{256,0},{1,257},{257,1},{2,258},{258,2},{3,259},{259,3},{4... | collective-permute-start | bytes 393224 | tf_op jit(solution)/shard_map/ppermute | solution.py:17
  602.7 3.2 collective-permute-start.21
  605.9 7.4 %collective-permute-start.22 = (bf16[2,2,2,64,128]{4,3,0,2,1:T(8,128)(2,1)S(1)}, bf16[2,2,2,64,128]{4,3,0,2,1:T(8,128)(2,1)S(1)}, u32[]{:S(2)}, u32[]{:S(2)}) collective-permute-start(bf16[2,2,2,64,128]{4,3,0,2,1:T(8,128)(2,1)S(1)} %collective-permute-done.21), channel_id=1, source_target_pairs={{0,4},{4,0},{2,6},{6,2},{8,12},{12,8},{10,14},{14,10},{16,20},{20,... | collective-permute-start | bytes 393224 | tf_op jit(solution)/shard_map/ppermute | solution.py:17
  613.4 10.3 %collective-permute-start.23 = (bf16[2,2,2,64,128]{4,3,0,2,1:T(8,128)(2,1)S(1)}, bf16[2,2,2,64,128]{4,3,0,2,1:T(8,128)(2,1)S(1)}, u32[]{:S(2)}, u32[]{:S(2)}) collective-permute-start(bf16[2,2,2,64,128]{4,3,0,2,1:T(8,128)(2,1)S(1)} %collective-permute-done.22), channel_id=1, source_target_pairs={{0,8},{8,0},{2,10},{10,2},{4,12},{12,4},{6,14},{14,6},{16,24},{24,... | collective-permute-start | bytes 393224 | tf_op jit(solution)/shard_map/ppermute | solution.py:17
  623.7 17.5 %collective-permute-start.24 = (bf16[2,2,2,64,128]{4,3,0,2,1:T(8,128)(2,1)S(1)}, bf16[2,2,2,64,128]{4,3,0,2,1:T(8,128)(2,1)S(1)}, u32[]{:S(2)}, u32[]{:S(2)}) collective-permute-start(bf16[2,2,2,64,128]{4,3,0,2,1:T(8,128)(2,1)S(1)} %collective-permute-done.23), channel_id=1, source_target_pairs={{0,16},{16,0},{2,18},{18,2},{4,20},{20,4},{6,22},{22,6},{8,24},{24... | collective-permute-start | bytes 393224 | tf_op jit(solution)/shard_map/ppermute | solution.py:17
  641.2 24.1 %collective-permute-start.25 = (bf16[2,2,2,64,128]{4,3,0,2,1:T(8,128)(2,1)S(1)}, bf16[2,2,2,64,128]{4,3,0,2,1:T(8,128)(2,1)S(1)}, u32[]{:S(2)}, u32[]{:S(2)}) collective-permute-start(bf16[2,2,2,64,128]{4,3,0,2,1:T(8,128)(2,1)S(1)} %collective-permute-done.24), channel_id=1, source_target_pairs={{0,32},{32,0},{2,34},{34,2},{4,36},{36,4},{6,38},{38,6},{8,40},{40... | collective-permute-start | bytes 393224 | tf_op jit(solution)/shard_map/ppermute | solution.py:17
  665.3 6.8 collective-permute-start.26
  672.1 8.4 %collective-permute-start.27 = (bf16[2,2,2,64,128]{4,3,0,2,1:T(8,128)(2,1)S(1)}, bf16[2,2,2,64,128]{4,3,0,2,1:T(8,128)(2,1)S(1)}, u32[]{:S(2)}, u32[]{:S(2)}) collective-permute-start(bf16[2,2,2,64,128]{4,3,0,2,1:T(8,128)(2,1)S(1)} %collective-permute-done.26), channel_id=1, source_target_pairs={{0,128},{128,0},{2,130},{130,2},{4,132},{132,4},{6,134},{134,6},{8... | collective-permute-start | bytes 393224 | tf_op jit(solution)/shard_map/ppermute | solution.py:17
  (58 other events, 541.1 us)
Sparse Core Ops, SparseCore 0:
  536.9 56.3 reduce-scatter.3
